TPU v7x, 256 devices: a whole 4x4x8 slice. The times are simulated.
256 devices in a mesh: row: 16 (over x_lo, y, core), col: 16 (over x_hi, z).
Axes of the slice: x: 4 (x_hi: 2, x_lo: 2; x = x_hi * 2 + x_lo), y: 4, z: 8, core: 2. Of those that a mesh axis runs over, the one named last changes fastest.
Arguments:
- tokens: bfloat16 [4096, 12288], P('row', 'col'), may hold values from -500 to 500
- ln_gain: bfloat16 [12288], P('col'), may hold values from 0.099609375 to 1.8984375
- ln_bias: bfloat16 [12288], P('col'), may hold values from -3 to 3
- weight: bfloat16 [12288, 18432], P('row', 'col'), may hold values from -0.0546875 to 0.0546875
Outputs:
- projected: bfloat16 [4096, 18432], P('row', 'col')
All inputs are finite; a program needn't handle non-finite values.
Results may differ from a plain program's by a relative error of at most 0.0049.
Values may be sent and summed in bfloat16 or wider, within the bound.
A program may use at most 128 MiB of HBM per device.

v0:
```python
import jax
import jax.numpy as jnp
from jax import lax
from jax.sharding import PartitionSpec as P

D = 12288


def on_device(tokens, ln_gain, ln_bias, weight):
    values = tokens.astype(jnp.float32)
    totals = lax.psum((jnp.sum(values, axis=1), jnp.sum(values * values, axis=1)), "col")
    mean = totals[0] / D
    var = totals[1] / D - mean * mean
    scale = lax.rsqrt(var + 1e-05)
    normed = (
        (values - mean[:, None]) * scale[:, None] * ln_gain.astype(jnp.float32)
        + ln_bias.astype(jnp.float32)
    ).astype(jnp.bfloat16)
    whole = lax.all_gather(normed, "col", axis=1, tiled=True)
    accum = jnp.dot(
        whole, lax.all_gather(weight, "row", axis=0, tiled=True), preferred_element_type=jnp.float32
    )
    return accum.astype(jnp.bfloat16)


def solution(mesh):
    in_specs = (P("row", "col"), P("col"), P("col"), P("row", "col"))
    out_specs = P("row", "col")
    return jax.shard_map(
        on_device, mesh=mesh, in_specs=in_specs, out_specs=out_specs, check_vma=False
    )
```

profile of v0, /device:TPU:1, one launch (start us, length us, event | category | flops | bytes accessed | tf_op | source)
XLA Modules:
  0.0 338.5 jit_solution(16274047731675112597)
XLA Ops:
  6.5 0.0 all-gather.3.cloned.1.call-start
  6.5 1.2 convert_reduce_fusion
  7.8 0.7 convert_element_type.16
  8.4 0.7 convert_element_type.17
  9.1 38.5 %all-reduce = (f32[256]{0:T(256)S(1)}, f32[256]{0:T(256)S(1)}) all-reduce(f32[256]{0:T(256)S(1)} %get-tuple-element.6, f32[256]{0:T(256)S(1)} %get-tuple-element.5), channel_id=1, replica_groups=mesh['row'=16,'col'=16] {'col'}, use_global_device_ids=true, to_apply=%region_3.0 | all-reduce | flops 512 | bytes 4096 | tf_op jit(solution)/shard_map/psum | solution.py:11
  47.7 2.0 fusion.3
  49.7 0.0 all-gather.3.cloned.1.call-update
  49.7 0.0 all-gather.5.cloned.1.call-start
  49.7 0.7 all-gather.5.cloned.1.call-update
  50.4 115.7 %all-gather.3.cloned.1.call-done = bf16[256,12288]{1,0:T(8,128)(2,1)} async-done(((bf16[256,768]{1,0:T(8,128)(2,1)}), bf16[256,12288]{1,0:T(8,128)(2,1)}) %all-gather.3.cloned.1.call-update) | async-done | bytes 6291472 | tf_op jit(solution)/shard_map/all_gather | solution.py:19
  166.1 149.6 %all-gather.5.cloned.1.call-done = bf16[12288,1152]{1,0:T(8,128)(2,1)} async-done(((bf16[768,1152]{1,0:T(8,128)(2,1)}), bf16[12288,1152]{1,0:T(8,128)(2,1)}) %all-gather.5.cloned.1.call-update) | async-done | bytes 28311568 | tf_op jit(solution)/shard_map/all_gather | solution.py:21
  315.7 16.0 %convolution_convert_fusion = bf16[256,1152]{1,0:T(8,128)(2,1)} fusion(bf16[256,12288]{1,0:T(8,128)(2,1)} %all-gather.3.cloned.1.call-done, bf16[12288,1152]{1,0:T(8,128)(2,1)} %all-gather.5.cloned.1.call-done), kind=kOutput, calls=%fused_computation | convolution fusion | flops 7248052224 | bytes 35192832 | tf_op jit(solution)/shard_map/dot_general | solution.py:20
  (1 shorter events, 0.0 us)
Async XLA Ops:
  6.5 159.6 %all-gather.3.cloned.1.call-start = ((), (), s32[]{:S(2)}) async-start(), calls=%async_computation | async-start | bytes 6684672 | tf_op jit(solution)/shard_map/all_gather | solution.py:19
  49.7 266.0 %all-gather.5.cloned.1.call-start = ((), (), s32[]{:S(2)}) async-start(), calls=%async_computation.1 | async-start | bytes 30081024 | tf_op jit(solution)/shard_map/all_gather | solution.py:21
Sparse Core Ops, SparseCore 0:
  49.8 116.2 all-gather.2
  167.9 147.7 all-gather.4
where the time goes:
time: 339 us
  waiting for transfers between devices  266 us (78%)
  blocking collectives  38.5 us (11%)
  matrix products  16 us (5%)
  between operations  13.4 us (4%)
  other arithmetic  4.6 us (1%)
    all_gather x1, waiting for transfers between devices, on_device(): lax.all_gather(weight, 'row', axis=0, tiled=True)  150 us
    all_gather x1, waiting for transfers between devices, on_device(): whole = lax.all_gather(normed, 'col', axis=1, tiled=True)  116 us
    psum x1, blocking collectives, on_device(): lax.psum((jnp.sum(values, axis=1), jnp.sum(values * values, axis=1)), 'col')  38.5 us
    dot_general x1, matrix products, on_device(): jnp.dot(whole, lax.all_gather(weight, 'row', axis=0, tiled=True), preferr...  16 us
  transfers between devices with their start and end apart: 2, of which 2 were waited for; matrix products, arithmetic and copies ran while one was open for 0% of the time, Pallas kernels for 0%

commit v1 on v0

v1 whole, which is shorter than its diff:
```python
import jax
import jax.numpy as jnp
from jax import lax
from jax.experimental import pallas as pl
from jax.experimental.pallas import tpu as pltpu
from jax.sharding import PartitionSpec as P

MESH = pl.DeviceIdType.MESH
D = 12288
TOK, FEAT, COLS = 256, 768, 1152
PIECE = 128
HALF = FEAT // 2
CHUNKS = ((0, 384), (384, 384), (768, 384))
NC = len(CHUNKS)
YN, ZN, XN = 4, 8, 4
SUB = 256


def kernel(tok, gain, bias, w, out, xs, relay, nm, wb0, wb1, wb2, tiles, stat, acc, rs_send, rs_recv,
           bx_s, ax_s, v0_r, v1_r, rl_r, zs_s, zs_r, ys_s, ys_r, dd_s, dd_r, lw_s, tz_s, tz_r, tx_s, tx_r, rs_s, rs_r):
    wb = (wb0, wb1, wb2)
    row, col = lax.axis_index("row"), lax.axis_index("col")
    core, y, x_lo = row % 2, (row // 2) % YN, row // 8
    z, x_hi = col % ZN, col // ZN
    x = 2 * x_hi + x_lo

    def at(x_hi=x_hi, x_lo=x_lo, y=y, z=z, core=core):
        return ((x_lo * YN + y) * 2 + core, x_hi * ZN + z)

    up, down = at(z=(z + 1) % ZN), at(z=(z + ZN - 1) % ZN)
    fore, back = at(y=(y + 1) % YN), at(y=(y + YN - 1) % YN)
    near = at(x_lo=1 - x_lo)
    over = at(x_hi=1 - x_hi, x_lo=1 - x_lo)
    opp = at(x_hi=1 - x_hi)
    twin = at(core=1 - core)
    zpeer = [None] + [at(z=(z + k) % ZN) for k in range(1, ZN)]
    xpeer = [None, near, over, opp]
    edge = x_lo == x_hi

    def send(src, dst, ssem, rsem, where):
        return pltpu.make_async_remote_copy(src_ref=src, dst_ref=dst, send_sem=ssem, recv_sem=rsem, device_id=where,
                                            device_id_type=MESH)

    barrier = pltpu.get_barrier_semaphore()
    partners = [*zpeer[1:], *xpeer[1:], fore, back, twin]
    for where in partners:
        pl.semaphore_signal(barrier, inc=1, device_id=where, device_id_type=MESH)
    pl.semaphore_wait(barrier, len(partners))

    def y_rows(dirn, k):
        half = (0, 1, 0)[k] if dirn == 0 else (1, 0, 1)[k]
        return pl.ds(half * HALF, HALF)

    def y_copy(dirn, c, k, arriving=False):
        hops = (1 if arriving else 0) + (1 if k == 2 else 0)
        owner = (y + YN - hops) % YN if dirn == 0 else (y + hops) % YN
        rows = y_rows(dirn, k)
        dst = wb[c].at[2 * owner + core, rows]
        src = dst
        if k < 2 and not arriving:
            start, size = CHUNKS[c]
            src = w.at[rows, pl.ds(start, size)]
        return send(src, dst, ys_s.at[dirn, c * 3 + k], ys_r.at[dirn, c * 3 + k], fore if dirn == 0 else back)

    def d_copy(c, i, arriving=False):
        owner = (y, (y + YN - 1) % YN, (y + 1) % YN, (y + 2) % YN)[i]
        dst = wb[c].at[2 * owner + ((1 - core) if arriving else core)]
        src = dst
        if i == 0 and not arriving:
            start, size = CHUNKS[c]
            src = w.at[:, pl.ds(start, size)]
        return send(src, dst, dd_s.at[c * 4 + i], dd_r.at[c * 4 + i], twin)

    def own_w(c):
        start, size = CHUNKS[c]
        return pltpu.make_async_copy(w.at[:, pl.ds(start, size)], wb[c].at[2 * y + core], lw_s.at[c])

    def rows_of(p):
        return pl.ds(p * PIECE, PIECE)

    def z_copy(dirn, v, s, p, arriving=False):
        hops = s + (1 if arriving else 0)
        block = (z + ZN - hops) % ZN if dirn == 0 else (z + hops) % ZN
        ref = xs.at[block, v, rows_of(p)]
        k = v * 8 + s * 2 + p
        return send(ref, ref, zs_s.at[dirn, k], zs_r.at[dirn, k], up if dirn == 0 else down)

    def to_over(p, edge_case):
        dst = relay.at[rows_of(p)] if edge_case else xs.at[z, 0, rows_of(p)]
        return send(tok.at[rows_of(p)], dst, bx_s.at[p], (rl_r if edge_case else v0_r).at[p], over)

    def to_near(p, edge_case):
        src = relay.at[rows_of(p)] if edge_case else tok.at[rows_of(p)]
        dst = xs.at[z, 1 if edge_case else 0, rows_of(p)]
        return send(src, dst, ax_s.at[p], (v1_r if edge_case else v0_r).at[p], near)

    def keep(p):
        return pltpu.make_async_copy(tok.at[rows_of(p)], xs.at[z, 1, rows_of(p)], v1_r.at[p])

    @pl.when(edge)
    def _():
        for p in range(2):
            to_over(p, True).start()
            keep(p).start()

    @pl.when(jnp.logical_not(edge))
    def _():
        for p in range(2):
            to_over(p, False).start()
            to_near(p, False).start()

    for k in range(2):
        for dirn in range(2):
            y_copy(dirn, 0, k).start()
    d_copy(0, 0).start()
    for c in range(NC):
        own_w(c).start()

    ones = jnp.ones((8, FEAT), jnp.bfloat16)
    over_lanes = (((1,), (1,)), ((), ()))
    values = tok[...]
    wide = values.astype(jnp.float32)
    square = wide * wide
    high = square.astype(jnp.bfloat16)
    low = (square - high.astype(jnp.float32)).astype(jnp.bfloat16)
    total = lax.dot_general(ones, values, over_lanes, preferred_element_type=jnp.float32)
    squares = lax.dot_general(ones, high, over_lanes, preferred_element_type=jnp.float32)
    squares += lax.dot_general(ones, low, over_lanes, preferred_element_type=jnp.float32)
    tiles[x, z, 0:1] = total[0:1]
    tiles[x, z, 1:2] = squares[0:1]
    for j in range(3):
        tiles[x, z, 2 + j:3 + j] = gain[:, j * SUB:(j + 1) * SUB].astype(jnp.float32)
        tiles[x, z, 5 + j:6 + j] = bias[:, j * SUB:(j + 1) * SUB].astype(jnp.float32)

    def tile_z(k):
        return send(tiles.at[x, z], tiles.at[x, z], tz_s.at[k], tz_r.at[k], zpeer[k])

    def tile_z_in(k):
        ref = tiles.at[x, (z + ZN - k) % ZN]
        return send(ref, ref, tz_s.at[k], tz_r.at[k], zpeer[k])

    x_of = (x, 2 * x_hi + 1 - x_lo, 2 * (1 - x_hi) + 1 - x_lo, 2 * (1 - x_hi) + x_lo)

    def tile_x(k, arriving=False):
        ref = tiles.at[x_of[k] if arriving else x]
        return send(ref, ref, tx_s.at[k], tx_r.at[k], xpeer[k])

    for k in range(1, ZN):
        tile_z(k).start()
    for k in range(1, ZN):
        tile_z_in(k).wait_recv()
    for k in range(1, XN):
        tile_x(k).start()

    def z_first(v, p):
        for dirn in range(2):
            z_copy(dirn, v, 0, p).start()

    def v0_arrive(p):
        to_near(p, False).wait_recv()

    def v1_arrive(p):
        to_near(p, True).wait_recv()

    def relay_on(p):
        @pl.when(edge)
        def _():
            to_over(p, True).wait_recv()
            to_near(p, True).start()

    def y_tick(c, k):
        for dirn in range(2):
            y_copy(dirn, c, k, arriving=True).wait_recv()
        if k == 0:
            for dirn in range(2):
                y_copy(dirn, c, 2).start()
        if k < 2 and c + 1 < NC:
            for dirn in range(2):
                y_copy(dirn, c + 1, k).start()
        if k == 1:
            d_copy(c, 1).start()
            d_copy(c, 2).start()
            if c + 1 < NC:
                d_copy(c + 1, 0).start()
        if k == 2:
            d_copy(c, 3).start()

    def normalize(block, v, p):
        lanes = 2 * v
        mean = stat[p * PIECE:(p + 1) * PIECE, lanes:lanes + 1]
        scale = stat[p * PIECE:(p + 1) * PIECE, lanes + 1:lanes + 2]
        for j in range(3):
            g = tiles[2 * x_lo, block, 2 + j:3 + j]
            b = tiles[2 * x_lo, block, 5 + j:6 + j]
            part = xs[block, v, p * PIECE:(p + 1) * PIECE, j * SUB:(j + 1) * SUB].astype(jnp.float32)
            nm[v, block, p * PIECE:(p + 1) * PIECE, j * SUB:(j + 1) * SUB] = (
                (part - mean) * scale * g + b).astype(jnp.bfloat16)

    def z_tick(v, s, p):
        arrivals = []
        if s < 3:
            arrivals = [0, 1]
        elif p == 0:
            arrivals = [0]
        else:
            arrivals = [1]
        for dirn in arrivals:
            z_copy(dirn, v, s, p, arriving=True).wait_recv()
            if s < 2 or (s == 2 and p == dirn):
                z_copy(dirn, v, s + 1, p).start()
        for dirn in arrivals:
            block = (z + ZN - s - 1) % ZN if dirn == 0 else (z + s + 1) % ZN
            normalize(block, v, p)

    def product(v, c):
        size = CHUNKS[c][1]
        acc[:, :size] = jnp.dot(nm[v, 0], wb[c][0], preferred_element_type=jnp.float32)

        def add(k, carry):
            acc[:, :size] += jnp.dot(nm[v, k], wb[c][k], preferred_element_type=jnp.float32)
            return carry

        lax.fori_loop(1, 2 * YN, add, 0)

    def rs(c):
        start, size = CHUNKS[c]
        cols = pl.ds(start, size)
        return send(rs_send.at[:, cols], rs_recv.at[:, cols], rs_s.at[c], rs_r.at[c], near)

    def give(c):
        start, size = CHUNKS[c]
        product(0, c)
        rs_send[:, start:start + size] = acc[:, :size].astype(jnp.bfloat16)
        rs(c).start()

    def finish(c):
        start, size = CHUNKS[c]
        product(1, c)
        rs(c).wait_recv()
        out[:, start:start + size] = (acc[:, :size] + rs_recv[:, start:start + size].astype(jnp.float32)).astype(jnp.bfloat16)

    def weights_ready(c):
        own_w(c).wait()
        for i in range(4):
            d_copy(c, i, arriving=True).wait_recv()

    v0_arrive(0)
    z_first(0, 0)
    relay_on(0)
    y_tick(0, 0)
    v0_arrive(1)
    z_first(0, 1)
    for k in range(1, XN):
        tile_x(k, arriving=True).wait_recv()
    means = []
    for lo in (1 - x_lo, x_lo):
        sums = jnp.zeros((8, SUB), jnp.float32)
        for hi in range(2):
            for zz in range(ZN):
                sums += tiles[2 * hi + lo, zz]
        mean = sums[0:1] / D
        var = sums[1:2] / D - mean * mean
        means += [mean, lax.rsqrt(var + 1e-05)]
    rows = jnp.concatenate(means + [jnp.zeros((124, SUB), jnp.float32)], axis=0)
    stat[...] = rows.T
    relay_on(1)
    for p in range(2):
        normalize(z, 0, p)
    y_tick(0, 1)
    z_tick(0, 0, 0)
    z_tick(0, 0, 1)
    z_tick(0, 1, 0)
    y_tick(0, 2)
    z_tick(0, 1, 1)
    y_tick(1, 0)
    v1_arrive(0)
    z_tick(0, 2, 0)
    z_first(1, 0)
    v1_arrive(1)
    z_tick(0, 2, 1)
    z_first(1, 1)
    y_tick(1, 1)
    z_tick(0, 3, 0)
    z_tick(0, 3, 1)
    for p in range(2):
        normalize(z, 1, p)
    weights_ready(0)
    give(0)
    y_tick(1, 2)
    z_tick(1, 0, 0)
    z_tick(1, 0, 1)
    y_tick(2, 0)
    weights_ready(1)
    give(1)
    z_tick(1, 1, 0)
    y_tick(2, 1)
    z_tick(1, 1, 1)
    z_tick(1, 2, 0)
    y_tick(2, 2)
    z_tick(1, 2, 1)
    weights_ready(2)
    give(2)
    z_tick(1, 3, 0)
    z_tick(1, 3, 1)
    for c in range(NC):
        finish(c)

    for p in range(2):
        to_over(p, False).wait_send()
        to_near(p, False).wait_send()
    for k in range(1, ZN):
        tile_z(k).wait_send()
    for k in range(1, XN):
        tile_x(k).wait_send()
    for dirn in range(2):
        for v in range(2):
            for s in range(4):
                for p in range(2):
                    if s < 3 or p == dirn:
                        z_copy(dirn, v, s, p).wait_send()
        for c in range(NC):
            for k in range(3):
                y_copy(dirn, c, k).wait_send()
    for c in range(NC):
        for i in range(4):
            d_copy(c, i).wait_send()
        rs(c).wait_send()


def on_device(tokens, ln_gain, ln_bias, weight):
    vmem = pl.BlockSpec(memory_space=pltpu.VMEM)
    hbm = pl.BlockSpec(memory_space=pl.ANY)
    dma = pltpu.SemaphoreType.DMA
    return pl.pallas_call(
        kernel,
        out_shape=jax.ShapeDtypeStruct((TOK, COLS), jnp.bfloat16),
        in_specs=[vmem, vmem, vmem, hbm],
        out_specs=vmem,
        scratch_shapes=[
            pltpu.VMEM((ZN, 2, TOK, FEAT), jnp.bfloat16),
            pltpu.VMEM((TOK, FEAT), jnp.bfloat16),
            pltpu.VMEM((2, ZN, TOK, FEAT), jnp.bfloat16),
            *[pltpu.VMEM((2 * YN, FEAT, size), jnp.bfloat16) for _, size in CHUNKS],
            pltpu.VMEM((XN, ZN, 8, SUB), jnp.float32),
            pltpu.VMEM((TOK, 128), jnp.float32),
            pltpu.VMEM((TOK, max(size for _, size in CHUNKS)), jnp.float32),
            pltpu.VMEM((TOK, COLS), jnp.bfloat16),
            pltpu.VMEM((TOK, COLS), jnp.bfloat16),
            dma((2,)), dma((2,)), dma((2,)), dma((2,)), dma((2,)),
            dma((2, 16)), dma((2, 16)),
            dma((2, 3 * NC)), dma((2, 3 * NC)),
            dma((4 * NC,)), dma((4 * NC,)),
            dma((NC,)),
            dma((ZN,)), dma((ZN,)), dma((XN,)), dma((XN,)),
            dma((NC,)), dma((NC,)),
        ],
        compiler_params=pltpu.CompilerParams(collective_id=0, has_side_effects=True, vmem_limit_bytes=56 * 1024 * 1024),
        cost_estimate=pl.CostEstimate(flops=2 * TOK * D * COLS, bytes_accessed=4 * 1024 * 1024, transcendentals=0),
    )(tokens, ln_gain.reshape(1, FEAT), ln_bias.reshape(1, FEAT), weight)


def solution(mesh):
    in_specs = (P("row", "col"), P("col"), P("col"), P("row", "col"))
    return jax.shard_map(on_device, mesh=mesh, in_specs=in_specs, out_specs=P("row", "col"), check_vma=False)
```

time: 339 us -> 94.3 us (0.28)
  waiting for transfers between devices: 266 us -> 0 us
  Pallas kernels: 0 us -> 89.6 us
  blocking collectives: 38.5 us -> 0 us
  matrix products: 16 us -> 0 us
  between operations: 13.4 us -> 0.01 us
  other arithmetic: 4.6 us -> 0 us
  local copies, waits for them, and re-layouts: 0 us -> 4.46 us
    all_gather x2 -> x0, waiting for transfers between devices: 265 us -> none  [the longest x1 150 us: on_device(): lax.all_gather(weight, 'row', axis=0, tiled=True)]
    pallas_call x0 -> x1, Pallas kernels: none -> 89.6 us  [on_device(): pl.pallas_call(kernel, out_shape=jax.ShapeDtypeStruct((TOK, COLS), jnp.bf...]
    psum x1 -> x0, blocking collectives: 38.5 us -> none  [on_device(): lax.psum((jnp.sum(values, axis=1), jnp.sum(values * values, axis=1)), 'col')]
    dot_general x1 -> x0, matrix products: 16 us -> none  [on_device(): jnp.dot(whole, lax.all_gather(weight, 'row', axis=0, tiled=True), preferr...]
  transfers between devices with their start and end apart: 2 -> 0, of which waited for: 2 -> 0; matrix products, arithmetic and copies ran while one was open for 0% -> 0% of each run, Pallas kernels for 0% -> 0%
where the time goes in v1:
time: 94.3 us; the launch traced here: 94.1 us
  Pallas kernels  89.6 us (95%)
  local copies, waits for them, and re-layouts  4.46 us (5%)
    pallas_call x1, Pallas kernels, on_device(): pl.pallas_call(kernel, out_shape=jax.ShapeDtypeStruct((TOK, COLS), jnp.bf...  89.6 us
    unnamed x1, local copies, waits for them, and re-layouts  1.92 us

profile of v1, /device:TPU:1, one launch (start us, length us, event | category | flops | bytes accessed | tf_op | source)
XLA Modules:
  0.0 94.1 jit_solution(5392506647874864436)
XLA Ops:
  0.0 1.3 %reshape.6.gain = bf16[1,768]{1,0:T(2,128)(2,1)} reshape(bf16[768]{0:T(1024)(128)(2,1)} %param.5) | data formatting | bytes 3072 | tf_op jit(solution)/shard_map/reshape | solution.py:359
  1.3 1.3 %reshape.7.bias = bf16[1,768]{1,0:T(2,128)(2,1)} reshape(bf16[768]{0:T(1024)(128)(2,1)} %param.6) | data formatting | bytes 3072 | tf_op jit(solution)/shard_map/reshape | solution.py:359
  2.5 89.6 %shard_map.46 = bf16[256,1152]{1,0:T(8,128)(2,1)} custom-call(bf16[256,768]{1,0:T(8,128)(2,1)} %tok.1, bf16[1,768]{1,0:T(2,128)(2,1)} %reshape.6.gain, bf16[1,768]{1,0:T(2,128)(2,1)} %reshape.7.bias, bf16[768,1152]{1,0:T(8,128)(2,1)} %w.1), custom_call_target="tpu_custom_call" | custom-call | flops 7247757312 | bytes 4194304 | tf_op jit(solution)/shard_map/pallas_call | solution.py:334
  92.1 1.9 %copy.6 = bf16[256,1152]{1,0:T(8,128)(2,1)} copy(bf16[256,1152]{1,0:T(8,128)(2,1)} %shard_map.46) | data formatting | bytes 1179648

commit v2 on v1

v2 whole, which is shorter than its diff:
```python
import jax
import jax.numpy as jnp
from jax import lax
from jax.experimental import pallas as pl
from jax.experimental.pallas import tpu as pltpu
from jax.sharding import PartitionSpec as P

MESH = pl.DeviceIdType.MESH
D = 12288
TOK, FEAT, COLS = 256, 768, 1152
PIECES = (4, 2)
HALF = FEAT // 2
CHUNKS = ((0, 512), (512, 256), (768, 256), (1024, 128))
NC = len(CHUNKS)
YN, ZN, XN = 4, 8, 4
SUB = 256


def kernel(tok, gain, bias, w, out, xs, relay, nm, wb0, wb1, wb2, wb3, tiles, stat, acc, rs_send, rs_recv,
           bx_s, ax_s, v0_r, v1_r, rl_r, zs_s, zs_r, ys_s, ys_r, dd_s, dd_r, lw_s, tz_s, tz_r, tx_s, tx_r, rs_s, rs_r):
    wb = (wb0, wb1, wb2, wb3)
    row, col = lax.axis_index("row"), lax.axis_index("col")
    core, y, x_lo = row % 2, (row // 2) % YN, row // 8
    z, x_hi = col % ZN, col // ZN
    x = 2 * x_hi + x_lo

    def at(x_hi=x_hi, x_lo=x_lo, y=y, z=z, core=core):
        return ((x_lo * YN + y) * 2 + core, x_hi * ZN + z)

    up, down = at(z=(z + 1) % ZN), at(z=(z + ZN - 1) % ZN)
    fore, back = at(y=(y + 1) % YN), at(y=(y + YN - 1) % YN)
    near = at(x_lo=1 - x_lo)
    over = at(x_hi=1 - x_hi, x_lo=1 - x_lo)
    opp = at(x_hi=1 - x_hi)
    twin = at(core=1 - core)
    zpeer = [None] + [at(z=(z + k) % ZN) for k in range(1, ZN)]
    xpeer = [None, near, over, opp]
    edge = x_lo == x_hi

    def send(src, dst, ssem, rsem, where):
        return pltpu.make_async_remote_copy(src_ref=src, dst_ref=dst, send_sem=ssem, recv_sem=rsem, device_id=where,
                                            device_id_type=MESH)

    barrier = pltpu.get_barrier_semaphore()
    partners = [*zpeer[1:], *xpeer[1:], fore, back, twin]
    for where in partners:
        pl.semaphore_signal(barrier, inc=1, device_id=where, device_id_type=MESH)
    pl.semaphore_wait(barrier, len(partners))

    def slot(y, core):
        rel = (2 * y + core + ZN - z) % ZN
        return 2 * rel + (rel // 4) * (15 - 4 * rel)

    def block_rows(y, core, start=0, size=FEAT):
        return pl.ds(pl.multiple_of(slot(y, core) * FEAT + start, 128), size)

    def y_copy(dirn, c, k, arriving=False):
        hops = (1 if arriving else 0) + (1 if k == 2 else 0)
        owner = (y + YN - hops) % YN if dirn == 0 else (y + hops) % YN
        half = ((0, 1, 0)[k] if dirn == 0 else (1, 0, 1)[k]) * HALF
        dst = wb[c].at[block_rows(owner, core, half, HALF)]
        src = dst
        if k < 2 and not arriving:
            start, size = CHUNKS[c]
            src = w.at[pl.ds(half, HALF), pl.ds(start, size)]
        return send(src, dst, ys_s.at[dirn, c * 3 + k], ys_r.at[dirn, c * 3 + k], fore if dirn == 0 else back)

    def d_copy(c, i, arriving=False):
        owner = (y, (y + YN - 1) % YN, (y + 1) % YN, (y + 2) % YN)[i]
        dst = wb[c].at[block_rows(owner, (1 - core) if arriving else core)]
        src = dst
        if i == 0 and not arriving:
            start, size = CHUNKS[c]
            src = w.at[:, pl.ds(start, size)]
        return send(src, dst, dd_s.at[c * 4 + i], dd_r.at[c * 4 + i], twin)

    def own_w(c):
        start, size = CHUNKS[c]
        return pltpu.make_async_copy(w.at[:, pl.ds(start, size)], wb[c].at[block_rows(y, core)], lw_s.at[c])

    def rows_of(v, p):
        size = TOK // PIECES[v]
        return pl.ds(p * size, size)

    def z_copy(dirn, v, s, p, arriving=False):
        hops = s + (1 if arriving else 0)
        block = (z + ZN - hops) % ZN if dirn == 0 else (z + hops) % ZN
        ref = xs.at[block, v, rows_of(v, p)]
        k = v * 16 + s * PIECES[v] + p
        return send(ref, ref, zs_s.at[dirn, k], zs_r.at[dirn, k], up if dirn == 0 else down)

    def to_over(p, edge_case):
        rows = rows_of(1 if edge_case else 0, p)
        dst = relay.at[rows] if edge_case else xs.at[z, 0, rows]
        return send(tok.at[rows], dst, bx_s.at[p], (rl_r if edge_case else v0_r).at[p], over)

    def to_near(p, edge_case):
        rows = rows_of(1 if edge_case else 0, p)
        src = relay.at[rows] if edge_case else tok.at[rows]
        dst = xs.at[z, 1 if edge_case else 0, rows]
        return send(src, dst, ax_s.at[p], (v1_r if edge_case else v0_r).at[p], near)

    def keep(p):
        rows = rows_of(1, p)
        return pltpu.make_async_copy(tok.at[rows], xs.at[z, 1, rows], v1_r.at[p])

    @pl.when(edge)
    def _():
        for p in range(PIECES[1]):
            to_over(p, True).start()
            keep(p).start()

    @pl.when(jnp.logical_not(edge))
    def _():
        for p in range(PIECES[0]):
            to_over(p, False).start()
            to_near(p, False).start()

    def y_own(c, k):
        for dirn in range(2):
            y_copy(dirn, c, k).start()

    y_own(0, 0)
    y_own(0, 1)
    y_own(1, 0)
    for c in range(NC):
        d_copy(c, 0).start()
        own_w(c).start()

    ones = jnp.ones((8, FEAT), jnp.bfloat16)
    over_lanes = (((1,), (1,)), ((), ()))
    values = tok[...]
    wide = values.astype(jnp.float32)
    square = wide * wide
    high = square.astype(jnp.bfloat16)
    low = (square - high.astype(jnp.float32)).astype(jnp.bfloat16)
    total = lax.dot_general(ones, values, over_lanes, preferred_element_type=jnp.float32)
    squares = lax.dot_general(ones, high, over_lanes, preferred_element_type=jnp.float32)
    squares += lax.dot_general(ones, low, over_lanes, preferred_element_type=jnp.float32)
    tiles[x, z, 0:1] = total[0:1]
    tiles[x, z, 1:2] = squares[0:1]
    for j in range(3):
        tiles[x, z, 2 + j:3 + j] = gain[j * SUB:(j + 1) * SUB].astype(jnp.float32).reshape(1, SUB)
        tiles[x, z, 5 + j:6 + j] = bias[j * SUB:(j + 1) * SUB].astype(jnp.float32).reshape(1, SUB)

    def tile_z(k):
        return send(tiles.at[x, z], tiles.at[x, z], tz_s.at[k], tz_r.at[k], zpeer[k])

    def tile_z_in(k):
        ref = tiles.at[x, (z + ZN - k) % ZN]
        return send(ref, ref, tz_s.at[k], tz_r.at[k], zpeer[k])

    x_of = (x, 2 * x_hi + 1 - x_lo, 2 * (1 - x_hi) + 1 - x_lo, 2 * (1 - x_hi) + x_lo)

    def tile_x(k, arriving=False):
        ref = tiles.at[x_of[k] if arriving else x]
        return send(ref, ref, tx_s.at[k], tx_r.at[k], xpeer[k])

    for k in range(1, ZN):
        tile_z(k).start()

    def z_first(v, p):
        for dirn in range(2):
            z_copy(dirn, v, 0, p).start()

    def v0_arrive(p):
        to_near(p, False).wait_recv()

    def v1_arrive(p):
        to_near(p, True).wait_recv()

    def relay_on(p):
        @pl.when(edge)
        def _():
            to_over(p, True).wait_recv()
            to_near(p, True).start()

    def y_tick(c, k, own=()):
        for dirn in range(2):
            y_copy(dirn, c, k, arriving=True).wait_recv()
        if k == 0:
            y_own(c, 2)
        for piece in own:
            y_own(*piece)
        if k == 1:
            d_copy(c, 1).start()
            d_copy(c, 2).start()
        if k == 2:
            d_copy(c, 3).start()

    def normalize(v, p, at, block):
        size = TOK // PIECES[v]
        rows = slice(p * size, (p + 1) * size)
        mean, scale = stat[rows, 2 * v:2 * v + 1], stat[rows, 2 * v + 1:2 * v + 2]
        for j in range(3):
            g = tiles[2 * x_lo, block, 2 + j:3 + j]
            b = tiles[2 * x_lo, block, 5 + j:6 + j]
            part = xs[block, v, rows, j * SUB:(j + 1) * SUB].astype(jnp.float32)
            nm[v, rows, at * FEAT + j * SUB:at * FEAT + (j + 1) * SUB] = ((part - mean) * scale * g + b).astype(jnp.bfloat16)

    def last_hop(dirn, v):
        half = PIECES[v] // 2
        return range(half) if dirn == 0 else range(half, 2 * half)

    def z_tick(v, s, p):
        arrivals = [0, 1]
        for dirn in arrivals:
            piece = last_hop(dirn, v)[p] if s == 3 else p
            z_copy(dirn, v, s, piece, arriving=True).wait_recv()
            if s < 2 or (s == 2 and piece in last_hop(dirn, v)):
                z_copy(dirn, v, s + 1, piece).start()
        for dirn in arrivals:
            piece = last_hop(dirn, v)[p] if s == 3 else p
            block = (z + ZN - s - 1) % ZN if dirn == 0 else (z + s + 1) % ZN
            normalize(v, piece, 7 if s == 3 else 2 * s + 1 + dirn, block)

    def product(v, c, first, last):
        k = slice(first * FEAT, last * FEAT)
        return jnp.dot(nm[v, :, k], wb[c][k], preferred_element_type=jnp.float32)

    def cols(c):
        start, size = CHUNKS[c]
        return slice(start, start + size)

    def rs(c):
        at = pl.ds(*CHUNKS[c])
        return send(rs_send.at[:, at], rs_recv.at[:, at], rs_s.at[c], rs_r.at[c], near)

    def give(c):
        own_w(c).wait()
        for i in range(4):
            d_copy(c, i, arriving=True).wait_recv()
        rs_send[:, cols(c)] = product(0, c, 0, ZN).astype(jnp.bfloat16)
        rs(c).start()

    for p in range(PIECES[0]):
        v0_arrive(p)
        z_first(0, p)
        if p == 1:
            for k in range(1, ZN):
                tile_z_in(k).wait_recv()
            for k in range(1, XN):
                tile_x(k).start()
            relay_on(0)
    for k in range(1, XN):
        tile_x(k, arriving=True).wait_recv()
    means = []
    for lo in (1 - x_lo, x_lo):
        sums = jnp.zeros((8, SUB), jnp.float32)
        for hi in range(2):
            for zz in range(ZN):
                sums += tiles[2 * hi + lo, zz]
        mean = sums[0:1] / D
        var = sums[1:2] / D - mean * mean
        means += [mean, lax.rsqrt(var + 1e-05)]
    stat[...] = jnp.concatenate(means + [jnp.zeros((124, SUB), jnp.float32)], axis=0).T
    z_tick(0, 0, 0)
    relay_on(1)
    z_tick(0, 0, 1)
    y_tick(0, 0, [(1, 1)])
    z_tick(0, 0, 2)
    z_tick(0, 0, 3)
    for p in range(PIECES[0]):
        normalize(0, p, 0, z)
    z_tick(0, 1, 0)
    z_tick(0, 1, 1)
    y_tick(0, 1, [(2, 0)])
    z_tick(0, 1, 2)
    z_tick(0, 1, 3)
    y_tick(1, 0, [(2, 1)])
    z_tick(0, 2, 0)
    z_tick(0, 2, 1)
    v1_arrive(0)
    z_first(1, 0)
    z_tick(0, 2, 2)
    z_tick(0, 2, 3)
    v1_arrive(1)
    z_first(1, 1)
    y_tick(0, 2, [(3, 0)])
    z_tick(0, 3, 0)
    z_tick(0, 3, 1)
    y_tick(1, 1, [(3, 1)])
    give(0)
    for p in range(PIECES[1]):
        normalize(1, p, 0, z)
    z_tick(1, 0, 0)
    y_tick(2, 0)
    z_tick(1, 0, 1)
    y_tick(1, 2)
    give(1)
    z_tick(1, 1, 0)
    y_tick(2, 1)
    y_tick(3, 0)
    z_tick(1, 1, 1)
    y_tick(3, 1)
    for c in range(2):
        acc[:, cols(c)] = product(1, c, 0, 5)
    z_tick(1, 2, 0)
    y_tick(2, 2)
    give(2)
    y_tick(3, 2)
    give(3)
    z_tick(1, 2, 1)
    for c in range(2):
        acc[:, cols(c)] += product(1, c, 5, 7)
    for c in range(2, NC):
        acc[:, cols(c)] = product(1, c, 0, 7)
    z_tick(1, 3, 0)
    for c in range(NC):
        rs(c).wait_recv()
        own = acc[:, cols(c)] + product(1, c, 7, ZN)
        out[:, cols(c)] = (own + rs_recv[:, cols(c)].astype(jnp.float32)).astype(jnp.bfloat16)

    @pl.when(edge)
    def _():
        for p in range(PIECES[1]):
            to_over(p, True).wait_send()
            to_near(p, True).wait_send()

    @pl.when(jnp.logical_not(edge))
    def _():
        for p in range(PIECES[0]):
            to_over(p, False).wait_send()
            to_near(p, False).wait_send()

    for k in range(1, ZN):
        tile_z(k).wait_send()
    for k in range(1, XN):
        tile_x(k).wait_send()
    for dirn in range(2):
        for v in range(2):
            for s in range(4):
                for p in range(PIECES[v]):
                    if s < 3 or p in last_hop(dirn, v):
                        z_copy(dirn, v, s, p).wait_send()
        for c in range(NC):
            for k in range(3):
                y_copy(dirn, c, k).wait_send()
    for c in range(NC):
        for i in range(4):
            d_copy(c, i).wait_send()
        rs(c).wait_send()


def on_device(tokens, ln_gain, ln_bias, weight):
    vmem = pl.BlockSpec(memory_space=pltpu.VMEM)
    hbm = pl.BlockSpec(memory_space=pl.ANY)
    dma = pltpu.SemaphoreType.DMA
    return pl.pallas_call(
        kernel,
        out_shape=jax.ShapeDtypeStruct((TOK, COLS), jnp.bfloat16),
        in_specs=[vmem, vmem, vmem, hbm],
        out_specs=vmem,
        scratch_shapes=[
            pltpu.VMEM((ZN, 2, TOK, FEAT), jnp.bfloat16),
            pltpu.VMEM((TOK, FEAT), jnp.bfloat16),
            pltpu.VMEM((2, TOK, ZN * FEAT), jnp.bfloat16),
            *[pltpu.VMEM((ZN * FEAT, size), jnp.bfloat16) for _, size in CHUNKS],
            pltpu.VMEM((XN, ZN, 8, SUB), jnp.float32),
            pltpu.VMEM((TOK, 128), jnp.float32),
            pltpu.VMEM((TOK, COLS), jnp.float32),
            pltpu.VMEM((TOK, COLS), jnp.bfloat16),
            pltpu.VMEM((TOK, COLS), jnp.bfloat16),
            dma((4,)), dma((4,)), dma((4,)), dma((2,)), dma((2,)),
            dma((2, 24)), dma((2, 24)),
            dma((2, 3 * NC)), dma((2, 3 * NC)),
            dma((4 * NC,)), dma((4 * NC,)),
            dma((NC,)),
            dma((ZN,)), dma((ZN,)), dma((XN,)), dma((XN,)),
            dma((NC,)), dma((NC,)),
        ],
        compiler_params=pltpu.CompilerParams(collective_id=0, has_side_effects=True, vmem_limit_bytes=58 * 1024 * 1024),
        cost_estimate=pl.CostEstimate(flops=2 * TOK * D * COLS, bytes_accessed=4 * 1024 * 1024, transcendentals=0),
    )(tokens, ln_gain, ln_bias, weight)


def solution(mesh):
    in_specs = (P("row", "col"), P("col"), P("col"), P("row", "col"))
    return jax.shard_map(on_device, mesh=mesh, in_specs=in_specs, out_specs=P("row", "col"), check_vma=False)
```

time: 94.3 us -> 86.2 us (0.914)
  Pallas kernels: 89.6 us -> 83.6 us
  local copies, waits for them, and re-layouts: 4.46 us -> 1.92 us
    pallas_call x1, Pallas kernels: 89.6 us -> 83.6 us  [on_device(): pl.pallas_call(kernel, out_shape=jax.ShapeDtypeStruct((TOK, COLS), jnp.bf...]
    reshape x2 -> x0, local copies, waits for them, and re-layouts: 2.54 us -> none  [the longest x1 1.28 us: on_device(): ln_bias.reshape(1, FEAT)]
where the time goes in v2:
time: 86.2 us; the launch traced here: 85.5 us
  Pallas kernels  83.6 us (97%)
  local copies, waits for them, and re-layouts  1.92 us (2%)
    pallas_call x1, Pallas kernels, on_device(): pl.pallas_call(kernel, out_shape=jax.ShapeDtypeStruct((TOK, COLS), jnp.bf...  83.6 us
    unnamed x1, local copies, waits for them, and re-layouts  1.92 us

profile of v2, /device:TPU:1, one launch (start us, length us, event | category | flops | bytes accessed | tf_op | source)
XLA Modules:
  0.0 85.5 jit_solution(7785520369404168867)
XLA Ops:
  0.0 83.6 %shard_map.46 = bf16[256,1152]{1,0:T(8,128)(2,1)} custom-call(bf16[256,768]{1,0:T(8,128)(2,1)} %tok.1, bf16[768]{0:T(1024)(128)(2,1)} %gain.1, bf16[768]{0:T(1024)(128)(2,1)} %bias.1, bf16[768,1152]{1,0:T(8,128)(2,1)} %w.1), custom_call_target="tpu_custom_call" | custom-call | flops 7247757312 | bytes 4194304 | tf_op jit(solution)/shard_map/pallas_call | solution.py:349
  83.6 1.9 %copy.6 = bf16[256,1152]{1,0:T(8,128)(2,1)} copy(bf16[256,1152]{1,0:T(8,128)(2,1)} %shard_map.46) | data formatting | bytes 1179648

commit v3 on v2

v3 whole, which is shorter than its diff:
```python
import jax
import jax.numpy as jnp
from jax import lax
from jax.experimental import pallas as pl
from jax.experimental.pallas import tpu as pltpu
from jax.sharding import PartitionSpec as P

MESH = pl.DeviceIdType.MESH
D = 12288
TOK, FEAT, COLS = 256, 768, 1152
EARLY = 96
PIECES = (2, 2)
HALF = FEAT // 2
CHUNKS = ((0, 512), (512, 256), (768, 256), (1024, 128))
NC = len(CHUNKS)
YN, ZN, XN = 4, 8, 4
SUB = 256


def kernel(tok_in, gain, bias, w, out, xs, relay, zb, nm, wb0, wb1, wb2, wb3, tiles, stat, acc, ahead, result, tok, rs_send, rs_recv,
           bx_s, ax_s, v0_r, v1_r, rl_r, zs_s, zs_r, ys_s, ys_r, dd_s, dd_r, lw_s, tz_s, tz_r, tx_s, tx_r, rs_s, rs_r,
           er_s, er_r, eo_s, eo_r, en_s, en_r, out_s, tok_s):
    wb = (wb0, wb1, wb2, wb3)
    row, col = lax.axis_index("row"), lax.axis_index("col")
    core, y, x_lo = row % 2, (row // 2) % YN, row // 8
    z, x_hi = col % ZN, col // ZN
    x = 2 * x_hi + x_lo

    def at(x_hi=x_hi, x_lo=x_lo, y=y, z=z, core=core):
        return ((x_lo * YN + y) * 2 + core, x_hi * ZN + z)

    up, down = at(z=(z + 1) % ZN), at(z=(z + ZN - 1) % ZN)
    fore, back = at(y=(y + 1) % YN), at(y=(y + YN - 1) % YN)
    near = at(x_lo=1 - x_lo)
    over = at(x_hi=1 - x_hi, x_lo=1 - x_lo)
    twin = at(core=1 - core)
    edge = x_lo == x_hi
    edge_index = (x_lo + x_hi + 1) % 2

    def send(src, dst, ssem, rsem, where):
        return pltpu.make_async_remote_copy(src_ref=src, dst_ref=dst, send_sem=ssem, recv_sem=rsem, device_id=where,
                                            device_id_type=MESH)

    def slot(y, core):
        rel = (2 * y + core + ZN - z) % ZN
        return 2 * rel + (rel // 4) * (15 - 4 * rel)

    def block_rows(y, core, start=0, size=FEAT):
        return pl.ds(pl.multiple_of(slot(y, core) * FEAT + start, 128), size)

    tokens_in = pltpu.make_async_copy(tok_in, tok, tok_s)
    tokens_in.start()

    barrier = pltpu.get_barrier_semaphore()
    partners = [fore, back, near, over, twin] + [at(z=(z + k) % ZN) for k in range(1, ZN)]
    for where in partners:
        pl.semaphore_signal(barrier, inc=1, device_id=where, device_id_type=MESH)

    def own_w(c):
        start, size = CHUNKS[c]
        return pltpu.make_async_copy(w.at[:, pl.ds(start, size)], wb[c].at[block_rows(y, core)], lw_s.at[c])

    for c in range(NC):
        own_w(c).start()
    tokens_in.wait()
    zb[0, z] = tok[:EARLY]

    ones = jnp.ones((8, FEAT), jnp.bfloat16)
    over_lanes = (((1,), (1,)), ((), ()))
    values = tok[...]
    wide = values.astype(jnp.float32)
    square = wide * wide
    high = square.astype(jnp.bfloat16)
    low = (square - high.astype(jnp.float32)).astype(jnp.bfloat16)
    total = lax.dot_general(ones, values, over_lanes, preferred_element_type=jnp.float32)
    squares = lax.dot_general(ones, high, over_lanes, preferred_element_type=jnp.float32)
    squares += lax.dot_general(ones, low, over_lanes, preferred_element_type=jnp.float32)
    tiles[x, z, 0:1] = total[0:1]
    tiles[x, z, 1:2] = squares[0:1]
    for j in range(3):
        tiles[x, z, 2 + j:3 + j] = gain[j * SUB:(j + 1) * SUB].astype(jnp.float32).reshape(1, SUB)
        tiles[x, z, 5 + j:6 + j] = bias[j * SUB:(j + 1) * SUB].astype(jnp.float32).reshape(1, SUB)

    pl.semaphore_wait(barrier, len(partners))

    def y_copy(dirn, c, k, arriving=False):
        hops = (1 if arriving else 0) + (1 if k == 2 else 0)
        owner = (y + YN - hops) % YN if dirn == 0 else (y + hops) % YN
        half = ((0, 1, 0)[k] if dirn == 0 else (1, 0, 1)[k]) * HALF
        dst = wb[c].at[block_rows(owner, core, half, HALF)]
        src = dst
        if k < 2 and not arriving:
            start, size = CHUNKS[c]
            src = w.at[pl.ds(half, HALF), pl.ds(start, size)]
        return send(src, dst, ys_s.at[dirn, c * 3 + k], ys_r.at[dirn, c * 3 + k], fore if dirn == 0 else back)

    def d_copy(c, i, arriving=False):
        owner = (y, (y + YN - 1) % YN, (y + 1) % YN, (y + 2) % YN)[i]
        dst = wb[c].at[block_rows(owner, (1 - core) if arriving else core)]
        src = dst
        if i == 0 and not arriving:
            start, size = CHUNKS[c]
            src = w.at[:, pl.ds(start, size)]
        return send(src, dst, dd_s.at[c * 4 + i], dd_r.at[c * 4 + i], twin)

    def rows_of(v, p):
        size = (TOK - EARLY) // PIECES[v]
        return pl.ds(EARLY + p * size, size)

    def z_copy(dirn, v, s, p, arriving=False):
        hops = s + (1 if arriving else 0)
        block = (z + ZN - hops) % ZN if dirn == 0 else (z + hops) % ZN
        ref = xs.at[block, v, rows_of(v, p)]
        k = v * 16 + s * PIECES[v] + p
        return send(ref, ref, zs_s.at[dirn, k], zs_r.at[dirn, k], up if dirn == 0 else down)

    def block_at(i):
        if i == 0:
            return z
        return (z + ZN - (i + 1) // 2) % ZN if i % 2 else (z + i // 2) % ZN

    def early_z(dirn, s, q, arriving=False):
        hops = s + (1 if arriving else 0)
        block = (z + ZN - hops) % ZN if dirn == 0 else (z + hops) % ZN
        ref = zb.at[0, block, pl.ds(q * (EARLY // 2), EARLY // 2)]
        return send(ref, ref, er_s.at[dirn, 2 * s + q], er_r.at[dirn, 2 * s + q], up if dirn == 0 else down)

    def early_over(i):
        block = block_at(i)
        return send(zb.at[0, block], zb.at[1, block], eo_s.at[i], eo_r.at[i], over)

    def early_near(i):
        block = block_at(i)
        return send(zb.at[edge_index, block], zb.at[2, block], en_s.at[i], en_r.at[i], near)

    def early_tick(s):
        for dirn in range(2):
            for q in range(2):
                if s < 3 or q == dirn:
                    early_z(dirn, s, q, arriving=True).wait_recv()
                    if s < 2 or (s == 2 and q == dirn):
                        early_z(dirn, s + 1, q).start()
        for i in (7,) if s == 3 else (2 * s + 1, 2 * s + 2):
            early_over(i).start()

    def early_on(i):
        early_over(i).wait_recv()
        early_near(i).start()

    def to_over(p, edge_case):
        rows = rows_of(1 if edge_case else 0, p)
        dst = relay.at[rows] if edge_case else xs.at[z, 0, rows]
        return send(tok.at[rows], dst, bx_s.at[p], (rl_r if edge_case else v0_r).at[p], over)

    def to_near(p, edge_case):
        rows = rows_of(1 if edge_case else 0, p)
        src = relay.at[rows] if edge_case else tok.at[rows]
        dst = xs.at[z, 1 if edge_case else 0, rows]
        return send(src, dst, ax_s.at[p], (v1_r if edge_case else v0_r).at[p], near)

    def keep(p):
        rows = rows_of(1, p)
        return pltpu.make_async_copy(tok.at[rows], xs.at[z, 1, rows], v1_r.at[p])

    def tile_z(k, arriving=False):
        ref = tiles.at[x, (z + ZN - k) % ZN if arriving else z]
        return send(ref, ref, tz_s.at[k], tz_r.at[k], at(z=(z + k) % ZN))

    def tiles_in():
        for k in range(1, ZN):
            tile_z(k, arriving=True).wait_recv()
        for k in range(2):
            tile_x(k).start()
        early_over(0).start()

    def y_own(c, k):
        for dirn in range(2):
            y_copy(dirn, c, k).start()

    for k in range(1, ZN):
        tile_z(k).start()
    y_own(0, 0)
    @pl.when(edge)
    def _():
        for p in range(PIECES[1]):
            to_over(p, True).start()
            keep(p).start()

    @pl.when(jnp.logical_not(edge))
    def _():
        for p in range(PIECES[0]):
            to_over(p, False).start()
            to_near(p, False).start()

    y_own(0, 1)
    y_own(1, 0)
    for q in range(2):
        for dirn in range(2):
            early_z(dirn, 0, q).start()
    for c in range(NC):
        d_copy(c, 0).start()

    x_near, x_over, x_far = 2 * x_hi + 1 - x_lo, 2 * (1 - x_hi) + 1 - x_lo, 2 * (1 - x_hi) + x_lo

    def tile_x(k, arriving=False):
        ref = tiles.at[(x_near, x_over, x_far)[k] if arriving else (x, x, x_near)[k]]
        return send(ref, ref, tx_s.at[k], tx_r.at[k], near if k == 0 else over)

    def z_first(v, p):
        for dirn in range(2):
            z_copy(dirn, v, 0, p).start()

    def v0_arrive(p):
        to_near(p, False).wait_recv()

    def v1_arrive(p):
        to_near(p, True).wait_recv()

    def relay_on(p):
        @pl.when(edge)
        def _():
            to_over(p, True).wait_recv()
            to_near(p, True).start()

    def y_tick(c, k, own=()):
        for dirn in range(2):
            y_copy(dirn, c, k, arriving=True).wait_recv()
        for piece in own[:1]:
            y_own(*piece)
        if k == 0:
            y_own(c, 2)
        for piece in own[1:]:
            y_own(*piece)
        if k == 1:
            d_copy(c, 1).start()
            d_copy(c, 2).start()
        if k == 2:
            d_copy(c, 3).start()

    def normalize(v, rows, at, block, source):
        mean, scale = stat[rows, 2 * v:2 * v + 1], stat[rows, 2 * v + 1:2 * v + 2]
        for j in range(3):
            lanes = slice(j * SUB, (j + 1) * SUB)
            g = tiles[2 * x_lo, block, 2 + j:3 + j]
            b = tiles[2 * x_lo, block, 5 + j:6 + j]
            part = source[:, lanes].astype(jnp.float32)
            nm[v, rows, at * FEAT + j * SUB:at * FEAT + (j + 1) * SUB] = ((part - mean) * scale * g + b).astype(jnp.bfloat16)

    def normalize_piece(v, p, i):
        size = (TOK - EARLY) // PIECES[v]
        start = EARLY + p * size
        block = block_at(i)
        normalize(v, slice(start, start + size), i, block, xs.at[block, v, pl.ds(start, size)])

    def normalize_early(i):
        block = block_at(i)
        early_near(i).wait_recv()
        normalize(0, slice(0, EARLY), i, block, zb.at[1 + edge_index, block])
        normalize(1, slice(0, EARLY), i, block, zb.at[2 - 2 * edge_index, block])

    def last_hop(dirn, v):
        half = PIECES[v] // 2
        return range(half) if dirn == 0 else range(half, 2 * half)

    def z_move(v, s, p):
        for dirn in range(2):
            piece = last_hop(dirn, v)[p] if s == 3 else p
            z_copy(dirn, v, s, piece, arriving=True).wait_recv()
            if s < 2 or (s == 2 and piece in last_hop(dirn, v)):
                z_copy(dirn, v, s + 1, piece).start()

    def z_norm(v, s, p):
        for dirn in range(2):
            normalize_piece(v, last_hop(dirn, v)[p] if s == 3 else p, 7 if s == 3 else 2 * s + 1 + dirn)

    def product(v, c, first, last):
        k = slice(first * FEAT, last * FEAT)
        return jnp.dot(nm[v, :, k], wb[c][k], preferred_element_type=jnp.float32)

    def product_of(v, c, owners):
        total = None
        for owner in owners:
            for k in range(2):
                at = block_rows((y + owner) % YN, k)
                part = jnp.dot(nm[v, :, at], wb[c][at], preferred_element_type=jnp.float32)
                total = part if total is None else total + part
        return total

    def cols(c):
        start, size = CHUNKS[c]
        return slice(start, start + size)

    def rs(c):
        at = pl.ds(*CHUNKS[c])
        return send(rs_send.at[:, at], rs_recv.at[:, at], rs_s.at[c], rs_r.at[c], near)

    def weights(c, blocks):
        if 0 in blocks:
            own_w(c).wait()
        for i in blocks:
            d_copy(c, i, arriving=True).wait_recv()

    def before(c):
        weights(c, range(3))
        ahead[...] = product_of(0, c, (0, 3, 1))

    def give(c):
        if c == NC - 1:
            weights(c, (3,))
            part = ahead[...] + product_of(0, c, (2,))
        else:
            weights(c, range(4))
            part = product(0, c, 0, ZN)
        rs_send[:, cols(c)] = part.astype(jnp.bfloat16)
        rs(c).start()

    def part(c):
        acc[:, cols(c)] = product(1, c, 0, 5)

    def own(c):
        acc[:, cols(c)] = product(1, c, 0, ZN)

    def leave(c):
        at = pl.ds(*CHUNKS[c])
        return pltpu.make_async_copy(result.at[:, at], out.at[:, at], out_s.at[c])

    def final(c):
        total = acc[:, cols(c)]
        if c < NC - 2:
            total += product(1, c, 5, ZN)
        rs(c).wait_recv()
        result[:, cols(c)] = (total + rs_recv[:, cols(c)].astype(jnp.float32)).astype(jnp.bfloat16)
        leave(c).start()

    def enter(p):
        v0_arrive(p)
        z_first(0, p)

    def v1_first(p):
        v1_arrive(p)
        z_first(1, p)

    def tile_near():
        tile_x(0, arriving=True).wait_recv()
        tile_x(2).start()

    def statistics():
        tile_x(1, arriving=True).wait_recv()
        tile_x(2, arriving=True).wait_recv()
        means = []
        for lo in (1 - x_lo, x_lo):
            sums = jnp.zeros((8, SUB), jnp.float32)
            for hi in range(2):
                for zz in range(ZN):
                    sums += tiles[2 * hi + lo, zz]
            mean = sums[0:1] / D
            var = sums[1:2] / D - mean * mean
            means += [mean, lax.rsqrt(var + 1e-05)]
        stat[...] = jnp.concatenate(means + [jnp.zeros((124, SUB), jnp.float32)], axis=0).T

    def z_left(v):
        for dirn in range(2):
            for s in range(4):
                for p in range(PIECES[v]):
                    if s < 3 or p in last_hop(dirn, v):
                        z_copy(dirn, v, s, p).wait_send()

    def y_left(c):
        for dirn in range(2):
            for k in range(3):
                y_copy(dirn, c, k).wait_send()

    def drain(stage):
        if stage == 1:
            z_left(1)
            y_left(1)
            for c, i in ((0, 1), (0, 2), (0, 3), (1, 1), (1, 2), (1, 3)):
                d_copy(c, i).wait_send()
            rs(0).wait_send()
            return
        z_left(0)
        y_left(0)
        for c in range(NC):
            d_copy(c, 0).wait_send()
        for k in range(1, ZN):
            tile_z(k).wait_send()
        for k in range(3):
            tile_x(k).wait_send()
        for dirn in range(2):
            for s in range(4):
                for q in range(2):
                    if s < 3 or q == dirn:
                        early_z(dirn, s, q).wait_send()
        for i in range(ZN):
            early_over(i).wait_send()
            early_near(i).wait_send()

        @pl.when(edge)
        def _():
            for p in range(PIECES[1]):
                to_over(p, True).wait_send()
                to_near(p, True).wait_send()

        @pl.when(jnp.logical_not(edge))
        def _():
            for p in range(PIECES[0]):
                to_over(p, False).wait_send()
                to_near(p, False).wait_send()

    tiles_in()
    enter(0)
    relay_on(0)
    early_tick(0)
    enter(1)
    relay_on(1)
    tile_near()
    z_move(0, 0, 0)
    y_tick(0, 0, [(1, 1)])
    early_on(0)
    early_tick(1)
    early_on(1)
    z_move(0, 0, 1)
    early_on(2)
    z_move(0, 1, 0)
    y_tick(0, 1, [(2, 0)])
    statistics()
    z_norm(0, 0, 0)
    z_norm(0, 0, 1)
    early_tick(2)
    z_norm(0, 1, 0)
    normalize_piece(0, 0, 0)
    normalize_piece(0, 1, 0)
    early_on(3)
    y_tick(1, 0, [(2, 1)])
    normalize_early(0)
    z_move(0, 1, 1)
    z_norm(0, 1, 1)
    normalize_early(1)
    normalize_early(2)
    early_on(4)
    z_move(0, 2, 0)
    v1_first(0)
    y_tick(1, 1)
    z_norm(0, 2, 0)
    early_tick(3)
    early_on(5)
    normalize_early(3)
    normalize_piece(1, 0, 0)
    z_move(0, 2, 1)
    v1_first(1)
    z_norm(0, 2, 1)
    normalize_early(4)
    early_on(6)
    normalize_piece(1, 1, 0)
    normalize_early(5)
    early_on(7)
    y_tick(0, 2)
    z_move(0, 3, 0)
    z_move(1, 0, 0)
    z_norm(0, 3, 0)
    normalize_early(6)
    z_norm(1, 0, 0)
    z_move(1, 0, 1)
    z_norm(1, 0, 1)
    y_tick(2, 0, [(3, 0), (3, 1)])
    normalize_early(7)
    give(0)
    z_move(1, 1, 0)
    drain(0)
    z_move(1, 1, 1)
    y_tick(2, 1)
    z_norm(1, 1, 0)
    z_norm(1, 1, 1)
    part(0)
    z_move(1, 2, 0)
    y_tick(1, 2)
    z_norm(1, 2, 0)
    z_move(1, 2, 1)
    y_tick(3, 0)
    give(1)
    part(1)
    z_norm(1, 2, 1)
    z_move(1, 3, 0)
    y_tick(2, 2)
    drain(1)
    y_tick(3, 1)
    give(2)
    y_tick(3, 2)
    z_norm(1, 3, 0)
    own(2)
    before(3)
    give(3)
    own(3)
    final(0)
    final(1)
    final(2)
    final(3)

    for c in range(2, NC):
        y_left(c)
        for i in range(1, 4):
            d_copy(c, i).wait_send()
    for c in range(1, NC):
        rs(c).wait_send()
    for c in range(NC):
        leave(c).wait()


def on_device(tokens, ln_gain, ln_bias, weight):
    vmem = pl.BlockSpec(memory_space=pltpu.VMEM)
    hbm = pl.BlockSpec(memory_space=pl.ANY)
    dma = pltpu.SemaphoreType.DMA
    return pl.pallas_call(
        kernel,
        out_shape=jax.ShapeDtypeStruct((TOK, COLS), jnp.bfloat16),
        in_specs=[hbm, vmem, vmem, hbm],
        out_specs=hbm,
        scratch_shapes=[
            pltpu.VMEM((ZN, 2, TOK, FEAT), jnp.bfloat16),
            pltpu.VMEM((TOK, FEAT), jnp.bfloat16),
            pltpu.VMEM((3, ZN, EARLY, FEAT), jnp.bfloat16),
            pltpu.VMEM((2, TOK, ZN * FEAT), jnp.bfloat16),
            *[pltpu.VMEM((ZN * FEAT, size), jnp.bfloat16) for _, size in CHUNKS],
            pltpu.VMEM((XN, ZN, 8, SUB), jnp.float32),
            pltpu.VMEM((TOK, 128), jnp.float32),
            pltpu.VMEM((TOK, COLS), jnp.float32),
            pltpu.VMEM((TOK, CHUNKS[NC - 1][1]), jnp.float32),
            pltpu.VMEM((TOK, COLS), jnp.bfloat16),
            pltpu.VMEM((TOK, FEAT), jnp.bfloat16),
            pltpu.VMEM((TOK, COLS), jnp.bfloat16),
            pltpu.VMEM((TOK, COLS), jnp.bfloat16),
            dma((4,)), dma((4,)), dma((4,)), dma((2,)), dma((2,)),
            dma((2, 24)), dma((2, 24)),
            dma((2, 3 * NC)), dma((2, 3 * NC)),
            dma((4 * NC,)), dma((4 * NC,)),
            dma((NC,)),
            dma((ZN,)), dma((ZN,)), dma((3,)), dma((3,)),
            dma((NC,)), dma((NC,)),
            dma((2, 8)), dma((2, 8)), dma((ZN,)), dma((ZN,)), dma((ZN,)), dma((ZN,)),
            dma((NC,)), dma(()),
        ],
        compiler_params=pltpu.CompilerParams(collective_id=0, has_side_effects=True, vmem_limit_bytes=58 * 1024 * 1024),
        cost_estimate=pl.CostEstimate(flops=2 * TOK * D * COLS, bytes_accessed=4 * 1024 * 1024, transcendentals=0),
    )(tokens, ln_gain, ln_bias, weight)


def solution(mesh):
    in_specs = (P("row", "col"), P("col"), P("col"), P("row", "col"))
    return jax.shard_map(on_device, mesh=mesh, in_specs=in_specs, out_specs=P("row", "col"), check_vma=False)
```

time: 86.2 us -> 81.2 us (0.942)
  Pallas kernels: 83.6 us -> 79.1 us
    pallas_call x1, Pallas kernels: 83.6 us -> 79.1 us  [on_device(): pl.pallas_call(kernel, out_shape=jax.ShapeDtypeStruct((TOK, COLS), jnp.bf...]
where the time goes in v3:
time: 81.2 us; the launch traced here: 81 us
  Pallas kernels  79.1 us (97%)
  local copies, waits for them, and re-layouts  1.92 us (2%)
    pallas_call x1, Pallas kernels, on_device(): pl.pallas_call(kernel, out_shape=jax.ShapeDtypeStruct((TOK, COLS), jnp.bf...  79.1 us
    unnamed x1, local copies, waits for them, and re-layouts  1.92 us

profile of v3, /device:TPU:1, one launch (start us, length us, event | category | flops | bytes accessed | tf_op | source)
XLA Modules:
  0.0 81.0 jit_solution(1934776593561385688)
XLA Ops:
  0.0 79.1 %shard_map.46 = bf16[256,1152]{1,0:T(8,128)(2,1)} custom-call(bf16[256,768]{1,0:T(8,128)(2,1)} %tok_in.1, bf16[768]{0:T(1024)(128)(2,1)} %gain.1, bf16[768]{0:T(1024)(128)(2,1)} %bias.1, bf16[768,1152]{1,0:T(8,128)(2,1)} %w.1), custom_call_target="tpu_custom_call" | custom-call | flops 7247757312 | bytes 4194304 | tf_op jit(solution)/shard_map/pallas_call | solution.py:513
  79.1 1.9 %copy.6 = bf16[256,1152]{1,0:T(8,128)(2,1)} copy(bf16[256,1152]{1,0:T(8,128)(2,1)} %shard_map.46) | data formatting | bytes 1179648

commit v4 on v3

--- a/solution.py
+++ b/solution.py
@@ -19,7 +19,7 @@
 
 def kernel(tok_in, gain, bias, w, out, xs, relay, zb, nm, wb0, wb1, wb2, wb3, tiles, stat, acc, ahead, result, tok, rs_send, rs_recv,
            bx_s, ax_s, v0_r, v1_r, rl_r, zs_s, zs_r, ys_s, ys_r, dd_s, dd_r, lw_s, tz_s, tz_r, tx_s, tx_r, rs_s, rs_r,
-           er_s, er_r, eo_s, eo_r, en_s, en_r, out_s, tok_s):
+           er_s, er_r, eo_s, eo_r, en_s, en_r, out_s, tok_s, z_ready):
     wb = (wb0, wb1, wb2, wb3)
     row, col = lax.axis_index("row"), lax.axis_index("col")
     core, y, x_lo = row % 2, (row // 2) % YN, row // 8
@@ -51,10 +51,13 @@
     tokens_in = pltpu.make_async_copy(tok_in, tok, tok_s)
     tokens_in.start()
 
+    def signal(semaphore, where):
+        pl.semaphore_signal(semaphore, inc=1, device_id=where, device_id_type=MESH)
+
     barrier = pltpu.get_barrier_semaphore()
-    partners = [fore, back, near, over, twin] + [at(z=(z + k) % ZN) for k in range(1, ZN)]
-    for where in partners:
-        pl.semaphore_signal(barrier, inc=1, device_id=where, device_id_type=MESH)
+    even, odd = z % 2 == 0, z % 2 == 1
+    for where in (fore, back, near, over, twin):
+        signal(barrier, where)
 
     def own_w(c):
         start, size = CHUNKS[c]
@@ -62,8 +65,145 @@
 
     for c in range(NC):
         own_w(c).start()
+    @pl.when(even)
+    def _():
+        pl.semaphore_wait(barrier, 5)
+        signal(barrier, up)
+        signal(barrier, down)
+
+    @pl.when(odd)
+    def _():
+        pl.semaphore_wait(barrier, 7)
+        signal(z_ready.at[0], up)
+        signal(z_ready.at[0], down)
+
+    def y_copy(dirn, c, k, arriving=False):
+        hops = (1 if arriving else 0) + (1 if k == 2 else 0)
+        owner = (y + YN - hops) % YN if dirn == 0 else (y + hops) % YN
+        half = ((0, 1, 0)[k] if dirn == 0 else (1, 0, 1)[k]) * HALF
+        dst = wb[c].at[block_rows(owner, core, half, HALF)]
+        src = dst
+        if k < 2 and not arriving:
+            start, size = CHUNKS[c]
+            src = w.at[pl.ds(half, HALF), pl.ds(start, size)]
+        return send(src, dst, ys_s.at[dirn, c * 3 + k], ys_r.at[dirn, c * 3 + k], fore if dirn == 0 else back)
+
+    def d_copy(c, i, arriving=False):
+        owner = (y, (y + YN - 1) % YN, (y + 1) % YN, (y + 2) % YN)[i]
+        dst = wb[c].at[block_rows(owner, (1 - core) if arriving else core)]
+        src = dst
+        if i == 0 and not arriving:
+            start, size = CHUNKS[c]
+            src = w.at[:, pl.ds(start, size)]
+        return send(src, dst, dd_s.at[c * 4 + i], dd_r.at[c * 4 + i], twin)
+
+    def rows_of(v, p):
+        size = (TOK - EARLY) // PIECES[v]
+        return pl.ds(EARLY + p * size, size)
+
+    def z_copy(dirn, v, s, p, arriving=False):
+        hops = s + (1 if arriving else 0)
+        block = (z + ZN - hops) % ZN if dirn == 0 else (z + hops) % ZN
+        ref = xs.at[block, v, rows_of(v, p)]
+        k = v * 16 + s * PIECES[v] + p
+        return send(ref, ref, zs_s.at[dirn, k], zs_r.at[dirn, k], up if dirn == 0 else down)
+
+    def block_at(i):
+        if i == 0:
+            return z
+        return (z + ZN - (i + 1) // 2) % ZN if i % 2 else (z + i // 2) % ZN
+
+    def early_z(dirn, s, q, arriving=False):
+        hops = s + (1 if arriving else 0)
+        block = (z + ZN - hops) % ZN if dirn == 0 else (z + hops) % ZN
+        ref = zb.at[0, block, pl.ds(q * (EARLY // 2), EARLY // 2)]
+        return send(ref, ref, er_s.at[dirn, 2 * s + q], er_r.at[dirn, 2 * s + q], up if dirn == 0 else down)
+
+    def early_over(i):
+        block = block_at(i)
+        return send(zb.at[0, block], zb.at[1, block], eo_s.at[i], eo_r.at[i], over)
+
+    def early_near(i):
+        block = block_at(i)
+        return send(zb.at[edge_index, block], zb.at[2, block], en_s.at[i], en_r.at[i], near)
+
+    def early_tick(s):
+        for dirn in range(2):
+            for q in range(2):
+                if s < 3 or q == dirn:
+                    early_z(dirn, s, q, arriving=True).wait_recv()
+                    if s < 2 or (s == 2 and q == dirn):
+                        early_z(dirn, s + 1, q).start()
+        for i in (7,) if s == 3 else (2 * s + 1, 2 * s + 2):
+            early_over(i).start()
+
+    def early_on(i):
+        early_over(i).wait_recv()
+        early_near(i).start()
+
+    def to_over(p, edge_case):
+        rows = rows_of(1 if edge_case else 0, p)
+        dst = relay.at[rows] if edge_case else xs.at[z, 0, rows]
+        return send(tok.at[rows], dst, bx_s.at[p], (rl_r if edge_case else v0_r).at[p], over)
+
+    def to_near(p, edge_case):
+        rows = rows_of(1 if edge_case else 0, p)
+        src = relay.at[rows] if edge_case else tok.at[rows]
+        dst = xs.at[z, 1 if edge_case else 0, rows]
+        return send(src, dst, ax_s.at[p], (v1_r if edge_case else v0_r).at[p], near)
+
+    def keep(p):
+        rows = rows_of(1, p)
+        return pltpu.make_async_copy(tok.at[rows], xs.at[z, 1, rows], v1_r.at[p])
+
+    def tile_z(k, arriving=False):
+        ref = tiles.at[x, (z + ZN - k) % ZN if arriving else z]
+        return send(ref, ref, tz_s.at[k], tz_r.at[k], at(z=(z + k) % ZN))
+
+    def tiles_in():
+        for k in range(1, ZN):
+            tile_z(k, arriving=True).wait_recv()
+        for k in range(2):
+            tile_x(k).start()
+        early_over(0).start()
+
+    def y_own(c, k):
+        for dirn in range(2):
+            y_copy(dirn, c, k).start()
+
+    y_own(0, 0)
+    y_own(0, 1)
+    y_own(1, 0)
+    for c in range(NC):
+        d_copy(c, 0).start()
     tokens_in.wait()
+
+    @pl.when(edge)
+    def _():
+        for p in range(PIECES[1]):
+            to_over(p, True).start()
+            keep(p).start()
+
+    @pl.when(jnp.logical_not(edge))
+    def _():
+        for p in range(PIECES[0]):
+            to_over(p, False).start()
+            to_near(p, False).start()
+
     zb[0, z] = tok[:EARLY]
+
+    @pl.when(even)
+    def _():
+        pl.semaphore_wait(z_ready.at[0], 2)
+
+    def greet(k):
+        signal(z_ready.at[k], up)
+        signal(z_ready.at[k], down)
+
+    greet(1)
+    for q in range(2):
+        for dirn in range(2):
+            early_z(dirn, 0, q).start()
 
     ones = jnp.ones((8, FEAT), jnp.bfloat16)
     over_lanes = (((1,), (1,)), ((), ()))
@@ -80,125 +220,12 @@
     for j in range(3):
         tiles[x, z, 2 + j:3 + j] = gain[j * SUB:(j + 1) * SUB].astype(jnp.float32).reshape(1, SUB)
         tiles[x, z, 5 + j:6 + j] = bias[j * SUB:(j + 1) * SUB].astype(jnp.float32).reshape(1, SUB)
-
-    pl.semaphore_wait(barrier, len(partners))
-
-    def y_copy(dirn, c, k, arriving=False):
-        hops = (1 if arriving else 0) + (1 if k == 2 else 0)
-        owner = (y + YN - hops) % YN if dirn == 0 else (y + hops) % YN
-        half = ((0, 1, 0)[k] if dirn == 0 else (1, 0, 1)[k]) * HALF
-        dst = wb[c].at[block_rows(owner, core, half, HALF)]
-        src = dst
-        if k < 2 and not arriving:
-            start, size = CHUNKS[c]
-            src = w.at[pl.ds(half, HALF), pl.ds(start, size)]
-        return send(src, dst, ys_s.at[dirn, c * 3 + k], ys_r.at[dirn, c * 3 + k], fore if dirn == 0 else back)
-
-    def d_copy(c, i, arriving=False):
-        owner = (y, (y + YN - 1) % YN, (y + 1) % YN, (y + 2) % YN)[i]
-        dst = wb[c].at[block_rows(owner, (1 - core) if arriving else core)]
-        src = dst
-        if i == 0 and not arriving:
-            start, size = CHUNKS[c]
-            src = w.at[:, pl.ds(start, size)]
-        return send(src, dst, dd_s.at[c * 4 + i], dd_r.at[c * 4 + i], twin)
-
-    def rows_of(v, p):
-        size = (TOK - EARLY) // PIECES[v]
-        return pl.ds(EARLY + p * size, size)
-
-    def z_copy(dirn, v, s, p, arriving=False):
-        hops = s + (1 if arriving else 0)
-        block = (z + ZN - hops) % ZN if dirn == 0 else (z + hops) % ZN
-        ref = xs.at[block, v, rows_of(v, p)]
-        k = v * 16 + s * PIECES[v] + p
-        return send(ref, ref, zs_s.at[dirn, k], zs_r.at[dirn, k], up if dirn == 0 else down)
-
-    def block_at(i):
-        if i == 0:
-            return z
-        return (z + ZN - (i + 1) // 2) % ZN if i % 2 else (z + i // 2) % ZN
-
-    def early_z(dirn, s, q, arriving=False):
-        hops = s + (1 if arriving else 0)
-        block = (z + ZN - hops) % ZN if dirn == 0 else (z + hops) % ZN
-        ref = zb.at[0, block, pl.ds(q * (EARLY // 2), EARLY // 2)]
-        return send(ref, ref, er_s.at[dirn, 2 * s + q], er_r.at[dirn, 2 * s + q], up if dirn == 0 else down)
-
-    def early_over(i):
-        block = block_at(i)
-        return send(zb.at[0, block], zb.at[1, block], eo_s.at[i], eo_r.at[i], over)
-
-    def early_near(i):
-        block = block_at(i)
-        return send(zb.at[edge_index, block], zb.at[2, block], en_s.at[i], en_r.at[i], near)
-
-    def early_tick(s):
-        for dirn in range(2):
-            for q in range(2):
-                if s < 3 or q == dirn:
-                    early_z(dirn, s, q, arriving=True).wait_recv()
-                    if s < 2 or (s == 2 and q == dirn):
-                        early_z(dirn, s + 1, q).start()
-        for i in (7,) if s == 3 else (2 * s + 1, 2 * s + 2):
-            early_over(i).start()
-
-    def early_on(i):
-        early_over(i).wait_recv()
-        early_near(i).start()
-
-    def to_over(p, edge_case):
-        rows = rows_of(1 if edge_case else 0, p)
-        dst = relay.at[rows] if edge_case else xs.at[z, 0, rows]
-        return send(tok.at[rows], dst, bx_s.at[p], (rl_r if edge_case else v0_r).at[p], over)
-
-    def to_near(p, edge_case):
-        rows = rows_of(1 if edge_case else 0, p)
-        src = relay.at[rows] if edge_case else tok.at[rows]
-        dst = xs.at[z, 1 if edge_case else 0, rows]
-        return send(src, dst, ax_s.at[p], (v1_r if edge_case else v0_r).at[p], near)
-
-    def keep(p):
-        rows = rows_of(1, p)
-        return pltpu.make_async_copy(tok.at[rows], xs.at[z, 1, rows], v1_r.at[p])
-
-    def tile_z(k, arriving=False):
-        ref = tiles.at[x, (z + ZN - k) % ZN if arriving else z]
-        return send(ref, ref, tz_s.at[k], tz_r.at[k], at(z=(z + k) % ZN))
-
-    def tiles_in():
-        for k in range(1, ZN):
-            tile_z(k, arriving=True).wait_recv()
-        for k in range(2):
-            tile_x(k).start()
-        early_over(0).start()
-
-    def y_own(c, k):
-        for dirn in range(2):
-            y_copy(dirn, c, k).start()
-
+    for k in range(1, 4):
+        pl.semaphore_wait(z_ready.at[k], 2)
+        if k < 3:
+            greet(k + 1)
     for k in range(1, ZN):
         tile_z(k).start()
-    y_own(0, 0)
-    @pl.when(edge)
-    def _():
-        for p in range(PIECES[1]):
-            to_over(p, True).start()
-            keep(p).start()
-
-    @pl.when(jnp.logical_not(edge))
-    def _():
-        for p in range(PIECES[0]):
-            to_over(p, False).start()
-            to_near(p, False).start()
-
-    y_own(0, 1)
-    y_own(1, 0)
-    for q in range(2):
-        for dirn in range(2):
-            early_z(dirn, 0, q).start()
-    for c in range(NC):
-        d_copy(c, 0).start()
 
     x_near, x_over, x_far = 2 * x_hi + 1 - x_lo, 2 * (1 - x_hi) + 1 - x_lo, 2 * (1 - x_hi) + x_lo
 
@@ -314,20 +341,15 @@
         rs_send[:, cols(c)] = part.astype(jnp.bfloat16)
         rs(c).start()
 
-    def part(c):
-        acc[:, cols(c)] = product(1, c, 0, 5)
-
     def own(c):
-        acc[:, cols(c)] = product(1, c, 0, ZN)
+        acc[:, cols(c)] = product(1, c, 0, 7)
 
     def leave(c):
         at = pl.ds(*CHUNKS[c])
         return pltpu.make_async_copy(result.at[:, at], out.at[:, at], out_s.at[c])
 
     def final(c):
-        total = acc[:, cols(c)]
-        if c < NC - 2:
-            total += product(1, c, 5, ZN)
+        total = acc[:, cols(c)] + product(1, c, 7, ZN)
         rs(c).wait_recv()
         result[:, cols(c)] = (total + rs_recv[:, cols(c)].astype(jnp.float32)).astype(jnp.bfloat16)
         leave(c).start()
@@ -407,90 +429,90 @@
                 to_over(p, False).wait_send()
                 to_near(p, False).wait_send()
 
-    tiles_in()
     enter(0)
     relay_on(0)
-    early_tick(0)
     enter(1)
     relay_on(1)
+    tiles_in()
+    early_tick(0)
+    y_tick(0, 0, [(1, 1)])
+    z_move(0, 0, 0)
     tile_near()
-    z_move(0, 0, 0)
-    y_tick(0, 0, [(1, 1)])
+    z_move(0, 0, 1)
     early_on(0)
     early_tick(1)
+    y_tick(0, 1, [(2, 0)])
     early_on(1)
-    z_move(0, 0, 1)
+    z_move(0, 1, 0)
     early_on(2)
-    z_move(0, 1, 0)
-    y_tick(0, 1, [(2, 0)])
+    y_tick(1, 0, [(2, 1)])
+    z_move(0, 1, 1)
     statistics()
     z_norm(0, 0, 0)
     z_norm(0, 0, 1)
+    z_norm(0, 1, 0)
+    z_norm(0, 1, 1)
     early_tick(2)
-    z_norm(0, 1, 0)
+    y_tick(1, 1)
+    early_on(3)
     normalize_piece(0, 0, 0)
     normalize_piece(0, 1, 0)
-    early_on(3)
-    y_tick(1, 0, [(2, 1)])
     normalize_early(0)
-    z_move(0, 1, 1)
-    z_norm(0, 1, 1)
     normalize_early(1)
+    z_move(0, 2, 0)
+    early_on(4)
+    v1_first(0)
+    z_norm(0, 2, 0)
     normalize_early(2)
-    early_on(4)
-    z_move(0, 2, 0)
-    v1_first(0)
-    y_tick(1, 1)
-    z_norm(0, 2, 0)
-    early_tick(3)
-    early_on(5)
-    normalize_early(3)
     normalize_piece(1, 0, 0)
     z_move(0, 2, 1)
     v1_first(1)
     z_norm(0, 2, 1)
+    early_on(5)
+    normalize_early(3)
+    early_tick(3)
+    normalize_piece(1, 1, 0)
+    y_tick(0, 2)
+    early_on(6)
     normalize_early(4)
-    early_on(6)
-    normalize_piece(1, 1, 0)
-    normalize_early(5)
-    early_on(7)
-    y_tick(0, 2)
     z_move(0, 3, 0)
     z_move(1, 0, 0)
+    early_on(7)
+    y_tick(2, 0, [(3, 0), (3, 1)])
     z_norm(0, 3, 0)
+    normalize_early(5)
+    z_move(1, 0, 1)
+    z_norm(1, 0, 0)
+    z_norm(1, 0, 1)
     normalize_early(6)
-    z_norm(1, 0, 0)
-    z_move(1, 0, 1)
-    z_norm(1, 0, 1)
-    y_tick(2, 0, [(3, 0), (3, 1)])
+    z_move(1, 1, 0)
+    y_tick(2, 1)
+    z_norm(1, 1, 0)
     normalize_early(7)
     give(0)
-    z_move(1, 1, 0)
+    z_move(1, 1, 1)
+    y_tick(1, 2)
     drain(0)
-    z_move(1, 1, 1)
-    y_tick(2, 1)
-    z_norm(1, 1, 0)
+    y_tick(3, 0)
+    z_move(1, 2, 0)
+    give(1)
+    z_move(1, 2, 1)
     z_norm(1, 1, 1)
-    part(0)
-    z_move(1, 2, 0)
-    y_tick(1, 2)
     z_norm(1, 2, 0)
-    z_move(1, 2, 1)
-    y_tick(3, 0)
-    give(1)
-    part(1)
     z_norm(1, 2, 1)
+    y_tick(2, 2)
+    own(0)
+    y_tick(3, 1)
     z_move(1, 3, 0)
-    y_tick(2, 2)
-    drain(1)
-    y_tick(3, 1)
     give(2)
     y_tick(3, 2)
-    z_norm(1, 3, 0)
     own(2)
     before(3)
     give(3)
     own(3)
+    own(1)
+    drain(1)
+    z_norm(1, 3, 0)
     final(0)
     final(1)
     final(2)
@@ -537,7 +559,7 @@
             dma((ZN,)), dma((ZN,)), dma((3,)), dma((3,)),
             dma((NC,)), dma((NC,)),
             dma((2, 8)), dma((2, 8)), dma((ZN,)), dma((ZN,)), dma((ZN,)), dma((ZN,)),
-            dma((NC,)), dma(()),
+            dma((NC,)), dma(()), pltpu.SemaphoreType.REGULAR((4,)),
         ],
         compiler_params=pltpu.CompilerParams(collective_id=0, has_side_effects=True, vmem_limit_bytes=58 * 1024 * 1024),
         cost_estimate=pl.CostEstimate(flops=2 * TOK * D * COLS, bytes_accessed=4 * 1024 * 1024, transcendentals=0),

time: 81.2 us -> 80.7 us (level)
  no operation moved by 1% of the time
where the time goes in v4:
time: 80.7 us; the launch traced here: 80.3 us
  Pallas kernels  78.4 us (97%)
  local copies, waits for them, and re-layouts  1.92 us (2%)
    pallas_call x1, Pallas kernels, on_device(): pl.pallas_call(kernel, out_shape=jax.ShapeDtypeStruct((TOK, COLS), jnp.bf...  78.4 us
    unnamed x1, local copies, waits for them, and re-layouts  1.92 us

profile of v4, /device:TPU:1, one launch (start us, length us, event | category | flops | bytes accessed | tf_op | source)
XLA Modules:
  0.0 80.3 jit_solution(16910561833105772747)
XLA Ops:
  0.0 78.4 %shard_map.46 = bf16[256,1152]{1,0:T(8,128)(2,1)} custom-call(bf16[256,768]{1,0:T(8,128)(2,1)} %tok_in.1, bf16[768]{0:T(1024)(128)(2,1)} %gain.1, bf16[768]{0:T(1024)(128)(2,1)} %bias.1, bf16[768,1152]{1,0:T(8,128)(2,1)} %w.1), custom_call_target="tpu_custom_call" | custom-call | flops 7247757312 | bytes 4194304 | tf_op jit(solution)/shard_map/pallas_call | solution.py:535
  78.4 1.9 %copy.6 = bf16[256,1152]{1,0:T(8,128)(2,1)} copy(bf16[256,1152]{1,0:T(8,128)(2,1)} %shard_map.46) | data formatting | bytes 1179648

commit v5 on v4

--- a/solution.py
+++ b/solution.py
@@ -502,21 +502,21 @@
     z_norm(1, 2, 1)
     y_tick(2, 2)
     own(0)
+    own(1)
     y_tick(3, 1)
-    z_move(1, 3, 0)
     give(2)
     y_tick(3, 2)
     own(2)
     before(3)
     give(3)
     own(3)
-    own(1)
-    drain(1)
+    z_move(1, 3, 0)
     z_norm(1, 3, 0)
     final(0)
     final(1)
     final(2)
     final(3)
+    drain(1)
 
     for c in range(2, NC):
         y_left(c)

time: 80.7 us -> 79.7 us (0.988)
  Pallas kernels: 78.4 us -> 77.3 us
    pallas_call x1, Pallas kernels: 78.4 us -> 77.3 us  [on_device(): pl.pallas_call(kernel, out_shape=jax.ShapeDtypeStruct((TOK, COLS), jnp.bf...]
where the time goes in v5:
time: 79.7 us; the launch traced here: 79.2 us
  Pallas kernels  77.3 us (97%)
  local copies, waits for them, and re-layouts  1.92 us (2%)
    pallas_call x1, Pallas kernels, on_device(): pl.pallas_call(kernel, out_shape=jax.ShapeDtypeStruct((TOK, COLS), jnp.bf...  77.3 us
    unnamed x1, local copies, waits for them, and re-layouts  1.92 us

profile of v5, /device:TPU:1, one launch (start us, length us, event | category | flops | bytes accessed | tf_op | source)
XLA Modules:
  0.0 79.2 jit_solution(9936435504327365019)
XLA Ops:
  0.0 77.3 %shard_map.46 = bf16[256,1152]{1,0:T(8,128)(2,1)} custom-call(bf16[256,768]{1,0:T(8,128)(2,1)} %tok_in.1, bf16[768]{0:T(1024)(128)(2,1)} %gain.1, bf16[768]{0:T(1024)(128)(2,1)} %bias.1, bf16[768,1152]{1,0:T(8,128)(2,1)} %w.1), custom_call_target="tpu_custom_call" | custom-call | flops 7247757312 | bytes 4194304 | tf_op jit(solution)/shard_map/pallas_call | solution.py:535
  77.3 1.9 %copy.6 = bf16[256,1152]{1,0:T(8,128)(2,1)} copy(bf16[256,1152]{1,0:T(8,128)(2,1)} %shard_map.46) | data formatting | bytes 1179648
